TPU v7x, 32 devices: a whole 2x2x4 slice. The times are simulated.
32 devices in a mesh: dp: 4 (over x, core), row: 2 (over y), col: 4 (over z).
Axes of the slice: x: 2, y: 2, z: 4, core: 2. Of those that a mesh axis runs over, the one named last changes fastest.
Arguments:
- activations: bfloat16 [8192, 8192], P('dp', 'row'), may hold values from -24 to 24
- out_grads: bfloat16 [8192, 16384], P(('dp', 'row'), 'col'), may hold values from -24 to 24
- weights: float32 [16384, 8192], P(('col', 'dp'), 'row'), may hold values from -0.0625 to 0.0625
- momentum: bfloat16 [16384, 8192], P(('col', 'dp'), 'row'), may hold values from -3 to 3
- scores: float32 [16384, 8192], P(('col', 'dp'), 'row'), may hold values from -6 to 6
- row_moment: float32 [16384], P(('col', 'dp')), may hold values from 0.05 to 90
- col_moment: float32 [8192], P('row'), may hold values from 0.05 to 90
Outputs:
- weights_new: float32 [16384, 8192], P(('col', 'dp'), 'row')
- momentum_new: bfloat16 [16384, 8192], P(('col', 'dp'), 'row')
- scores_new: float32 [16384, 8192], P(('col', 'dp'), 'row')
- row_moment_new: float32 [16384], P(('col', 'dp'))
- col_moment_new: float32 [8192], P('row')
All inputs are finite; a program needn't handle non-finite values.
Results may differ from a plain program's by a relative error of at most 0.004.
Values may be sent and summed in bfloat16 or wider, within the bound.
A program may use at most 256 MiB of HBM per device.

v0:
```python
import math

import jax
import jax.numpy as jnp
from jax import lax
from jax.sharding import PartitionSpec as P

D = 8192
FF = 16384


def token_product(grad_rows, act_rows):
    return lax.dot_general(
        grad_rows, act_rows, (((0,), (0,)), ((), ())), preferred_element_type=jnp.float32
    )


def local(activations, out_grads, weights, momentum, scores, row_moment, col_moment):
    replicas = lax.axis_size("dp")
    token_scale = 1.0 / math.sqrt(activations.shape[0] * replicas)
    local_block = token_product(lax.all_gather(out_grads, "row", axis=0, tiled=True), activations)
    gradient = lax.psum_scatter(local_block, "dp", scatter_dimension=0, tiled=True) * token_scale
    squares = gradient * gradient + 1e-30
    row_part = jnp.sum(squares, axis=1)
    col_part = jnp.sum(squares, axis=0)
    row_full = lax.psum(row_part, "row")
    row_moment_new = 0.8 * row_moment + 0.2 * row_full / D
    col_full = lax.psum(col_part, ("dp", "col"))
    row_sum = lax.psum(jnp.sum(row_moment_new), ("dp", "col"))
    col_moment_new = 0.8 * col_moment + 0.2 * col_full / FF
    row_average = row_sum / FF
    update = gradient * lax.rsqrt(row_moment_new[:, None] * col_moment_new[None, :] / row_average)
    momentum_new = (0.9 * momentum.astype(jnp.float32) + 0.1 * update).astype(jnp.bfloat16)
    weights_new = weights - 0.01 * momentum_new.astype(jnp.float32)
    scores_new = scores - 50.0 * weights * gradient
    return (weights_new, momentum_new, scores_new, row_moment_new, col_moment_new)


def solution(mesh):
    return jax.shard_map(
        local,
        mesh=mesh,
        in_specs=(
            P("dp", "row"),
            P(("dp", "row"), "col"),
            P(("col", "dp"), "row"),
            P(("col", "dp"), "row"),
            P(("col", "dp"), "row"),
            P(("col", "dp")),
            P("row"),
        ),
        out_specs=(
            P(("col", "dp"), "row"),
            P(("col", "dp"), "row"),
            P(("col", "dp"), "row"),
            P(("col", "dp")),
            P("row"),
        ),
        check_vma=False,
    )
```

profile of v0, /device:TPU:0, one launch (start us, length us, event | category | flops | bytes accessed | tf_op | source)
XLA Modules:
  0.0 863.6 jit_solution(2938280889901366027)
XLA Ops:
  7.2 0.0 all-gather.2.cloned.1.call-start
  7.2 0.7 all-gather.2.cloned.1.call-update
  7.9 0.0 reduce-scatter.4.cloned.1.call-start
  7.9 203.2 %all-gather.2.cloned.1.call-done = bf16[2048,4096]{1,0:T(8,128)(2,1)} async-done(((bf16[1024,4096]{1,0:T(8,128)(2,1)}), bf16[2048,4096]{1,0:T(8,128)(2,1)}) %all-gather.2.cloned.1.call-update) | async-done | bytes 16777232 | tf_op jit(solution)/shard_map/all_gather | solution.py:21
  211.1 79.6 %fusion.3 = f32[4096,4096]{1,0:T(8,128)} fusion(bf16[2048,4096]{1,0:T(8,128)(2,1)} %all-gather.2.cloned.1.call-done, bf16[2048,4096]{1,0:T(8,128)(2,1)} %param.7), kind=kOutput, calls=%fused_computation.9 | convolution fusion | flops 68719476736 | bytes 100663296 | tf_op jit(solution)/shard_map/dot_general | solution.py:13
  290.8 0.0 reduce-scatter.4.cloned.1.call-update
  290.8 0.0 copy-start.3
  290.8 0.0 copy-start.2
  290.8 452.5 %reduce-scatter.4.cloned.1.call-done = f32[1024,4096]{1,0:T(8,128)} async-done(((f32[4096,4096]{1,0:T(8,128)}), f32[1024,4096]{1,0:T(8,128)}) %reduce-scatter.4.cloned.1.call-update) | async-done | bytes 16777232
  743.3 13.6 %fusion = (f32[4096]{0:T(1024)S(1)}, f32[1024]{0:T(1024)S(1)}) fusion(f32[1024,4096]{1,0:T(8,128)} %reduce-scatter.4.cloned.1.call-done), kind=kLoop, calls=%fused_computation.4 | loop fusion | flops 20966400 | bytes 16797696 | tf_op jit(solution)/shard_map/reduce_sum | solution.py:25
  756.9 4.9 psum.21
  761.9 0.0 copy-done.3
  761.9 0.6 fusion.2
  762.5 0.0 copy-start.1
  762.5 59.4 %all-reduce.1 = (f32[]{:T(128)}, f32[4096]{0:T(1024)S(1)}) all-reduce(f32[]{:T(128)} %get-tuple-element.11, f32[4096]{0:T(1024)S(1)} %get-tuple-element.5), channel_id=1, replica_groups=mesh['dp'=4,'row'=2,'col'=4] {'dp','col'}, use_global_device_ids=true, to_apply=%region_6.0 | all-reduce | flops 4097 | bytes 32776 | tf_op jit(solution)/shard_map/psum | solution.py:29
  822.5 0.0 copy-done.2
  822.6 0.0 copy-start
  822.6 34.2 %multiply_subtract_fusion.1 = (f32[1024,4096]{1,0:T(8,128)}, bf16[1024,4096]{1,0:T(8,128)(2,1)}, f32[1024,4096]{1,0:T(8,128)}) fusion(f32[1024,4096]{1,0:T(8,128)} %param.9, f32[]{:T(128)S(6)} %div.25, f32[4096]{0:T(1024)S(1)} %multiply_add_fusion.1, f32[1024]{0:T(1024)S(1)} %get-tuple-element.12, f32[1024,4096]{1,0:T(8,128)} %reduce-scatter.4.cloned.1.call-done, ...), kind=kLoop, calls=%fused_computation.1 | loop fusion | flops 62914560 | bytes 100683776 | tf_op jit(solution)/shard_map/sub | solution.py:34
  856.8 0.0 copy-done.1
  856.8 0.0 copy-done
  (1 shorter events, 0.0 us)
Async XLA Ops:
  7.2 204.0 %all-gather.2.cloned.1.call-start = ((), (), s32[]{:S(2)}) async-start(), calls=%async_computation.1 | async-start | bytes 25165824 | tf_op jit(solution)/shard_map/all_gather | solution.py:21
  7.9 735.4 %reduce-scatter.4.cloned.1.call-start = ((), (), s32[]{:S(2)}) async-start(), calls=%async_computation.2 | async-start | bytes 83886080
  290.8 471.1 %copy-start.3 = (f32[1024]{0:T(1024)S(1)}, f32[1024]{0:T(1024)}, u32[]{:S(2)}) copy-start(f32[1024]{0:T(1024)} %param.12) | copy-start | bytes 12292
  290.8 531.7 %copy-start.2 = (f32[4096]{0:T(1024)S(1)}, f32[4096]{0:T(1024)}, u32[]{:S(2)}) copy-start(f32[4096]{0:T(1024)} %param.13) | copy-start | bytes 49156
  762.5 94.3 %copy-start.1 = (f32[1024]{0:T(1024)}, f32[1024]{0:T(1024)S(1)}, u32[]{:S(2)}) copy-start(f32[1024]{0:T(1024)S(1)} %get-tuple-element.12) | copy-start | bytes 12292
  822.6 34.2 %copy-start = (f32[4096]{0:T(1024)}, f32[4096]{0:T(1024)S(1)}, u32[]{:S(2)}) copy-start(f32[4096]{0:T(1024)S(1)} %multiply_add_fusion.1) | copy-start | bytes 49156
Sparse Core Ops, SparseCore 0:
  9.5 201.5 all-gather.1
  290.9 452.3 reduce-scatter.3
where the time goes:
time: 864 us
  waiting for transfers between devices  656 us (76%)
  matrix products  79.6 us (9%)
  blocking collectives  64.4 us (7%)
  other arithmetic  48.4 us (6%)
  between operations  14.7 us (2%)
    unnamed x3, waiting for transfers between devices  453 us
    all_gather x1, waiting for transfers between devices, local(): lax.all_gather(out_grads, 'row', axis=0, tiled=True)  203 us
    dot_general x1, matrix products, token_product(): lax.dot_general(grad_rows, act_rows, (((0,), (0,)), ((), ())), preferred_...  79.6 us
    psum x1, blocking collectives, local(): row_sum = lax.psum(jnp.sum(row_moment_new), ('dp', 'col'))  59.4 us
    sub x1, other arithmetic, local(): weights_new = weights - 0.01 * momentum_new.astype(jnp.float32)  34.2 us
  transfers between devices with their start and end apart: 2, of which 2 were waited for; matrix products, arithmetic and copies ran while one was open for 0% of the time, Pallas kernels for 0%

commit v1 on v0

--- a/solution.py
+++ b/solution.py
@@ -7,6 +7,8 @@
 
 D = 8192
 FF = 16384
+
+PIECES = 4
 
 
 def token_product(grad_rows, act_rows):
@@ -18,17 +20,50 @@
 def local(activations, out_grads, weights, momentum, scores, row_moment, col_moment):
     replicas = lax.axis_size("dp")
     token_scale = 1.0 / math.sqrt(activations.shape[0] * replicas)
-    local_block = token_product(lax.all_gather(out_grads, "row", axis=0, tiled=True), activations)
-    gradient = lax.psum_scatter(local_block, "dp", scatter_dimension=0, tiled=True) * token_scale
-    squares = gradient * gradient + 1e-30
-    row_part = jnp.sum(squares, axis=1)
-    col_part = jnp.sum(squares, axis=0)
-    row_full = lax.psum(row_part, "row")
+    me = lax.axis_index("dp")
+    core = me % 2
+    same_chip = [(i, i ^ 1) for i in range(replicas)]
+    other_chip = [(i, i ^ 2) for i in range(replicas)]
+    block = out_grads.shape[1] // replicas
+    piece = block // PIECES
+
+    act_pair = lax.ppermute(activations, "dp", same_chip)
+
+    def columns(owner, j):
+        return lax.dynamic_slice_in_dim(out_grads, owner * block + j * piece, piece, 1)
+
+    def gathered(chip, j):
+        mine = columns(2 * chip + core, j)
+        theirs = lax.ppermute(columns(2 * chip + 1 - core, j), "dp", same_chip)
+        both = jnp.concatenate([mine, theirs], axis=1)
+        return lax.all_gather(both, "row", axis=0, tiled=True)
+
+    def chip_sum(chip, j):
+        both = gathered(chip, j)
+        return token_product(both[:, :piece], activations) + token_product(both[:, piece:], act_pair)
+
+    chip = me // 2
+    received = []
+    for j in range(PIECES):
+        partial = chip_sum(1 - chip, j).astype(jnp.bfloat16)
+        received.append(lax.ppermute(partial, "dp", other_chip))
+    gradients = []
+    row_parts = []
+    col_part = 0.0
+    for j in range(PIECES):
+        own = chip_sum(chip, j)
+        g = (own + received[j].astype(jnp.float32)) * token_scale
+        squares = g * g + 1e-30
+        gradients.append(g)
+        row_parts.append(jnp.sum(squares, axis=1))
+        col_part = col_part + jnp.sum(squares, axis=0)
+    row_full = lax.psum(jnp.concatenate(row_parts), "row")
     row_moment_new = 0.8 * row_moment + 0.2 * row_full / D
     col_full = lax.psum(col_part, ("dp", "col"))
     row_sum = lax.psum(jnp.sum(row_moment_new), ("dp", "col"))
     col_moment_new = 0.8 * col_moment + 0.2 * col_full / FF
     row_average = row_sum / FF
+    gradient = jnp.concatenate(gradients, axis=0)
     update = gradient * lax.rsqrt(row_moment_new[:, None] * col_moment_new[None, :] / row_average)
     momentum_new = (0.9 * momentum.astype(jnp.float32) + 0.1 * update).astype(jnp.bfloat16)
     weights_new = weights - 0.01 * momentum_new.astype(jnp.float32)

time: 864 us -> 474 us (0.55)
  waiting for transfers between devices: 656 us -> 159 us
  matrix products: 79.6 us -> 173 us
  starting transfers between devices: 0.08 us -> 10.6 us
    unnamed x3 -> x8, waiting for transfers between devices: 453 us -> 0.13 us
    dot_general x1 -> x16, matrix products: 79.6 us -> 173 us  [token_product(): lax.dot_general(grad_rows, act_rows, (((0,), (0,)), ((), ())), preferred_...]
    all_gather x1 -> x8, waiting for transfers between devices: 203 us -> 127 us  [gathered(): return lax.all_gather(both, 'row', axis=0, tiled=True)]
    ppermute x0 -> x13, waiting for transfers between devices: none -> 31.4 us  [the longest x8 31.4 us: gathered(): theirs = lax.ppermute(columns(2 * chip + 1 - core, j), 'dp', same_chip)]
    reduce_sum x1 -> x0, other arithmetic: 13.6 us -> none  [local(): col_part = jnp.sum(squares, axis=0)]
    ppermute x0 -> x13, starting transfers between devices: none -> 10.1 us  [the longest x4 6.34 us: local(): received.append(lax.ppermute(partial, 'dp', other_chip))]
    concatenate x0 -> x9, other arithmetic: none -> 9.46 us  [the longest x8 9.45 us: gathered(): both = jnp.concatenate([mine, theirs], axis=1)]
  transfers between devices with their start and end apart: 2 -> 21, of which waited for: 2 -> 16; matrix products, arithmetic and copies ran while one was open for 0% -> 38% of each run, Pallas kernels for 0% -> 0%
where the time goes in v1:
time: 474 us; the launch traced here: 471 us
  matrix products  173 us (36%)
  waiting for transfers between devices  159 us (34%)
  blocking collectives  65.3 us (14%)
  other arithmetic  42.7 us (9%)
  between operations  15.3 us (3%)
  starting transfers between devices  10.6 us (2%)
  local copies, waits for them, and re-layouts  5.64 us (1%)
    dot_general x16, matrix products, token_product(): lax.dot_general(grad_rows, act_rows, (((0,), (0,)), ((), ())), preferred_...  173 us
    all_gather x8, waiting for transfers between devices, gathered(): return lax.all_gather(both, 'row', axis=0, tiled=True)  127 us
    psum x1, blocking collectives, local(): row_sum = lax.psum(jnp.sum(row_moment_new), ('dp', 'col'))  60.4 us
    sub x1, other arithmetic, local(): weights_new = weights - 0.01 * momentum_new.astype(jnp.float32)  32.6 us
    ppermute x8, waiting for transfers between devices, gathered(): theirs = lax.ppermute(columns(2 * chip + 1 - core, j), 'dp', same_chip)  31.4 us
  transfers between devices with their start and end apart: 21, of which 16 were waited for; matrix products, arithmetic and copies ran while one was open for 38% of the time, Pallas kernels for 0%

profile of v1, /device:TPU:0, one launch (start us, length us, event | category | flops | bytes accessed | tf_op | source)
XLA Modules:
  0.0 471.0 jit_solution(3307684967046479038)
XLA Ops:
  7.2 0.5 collective-permute-start.1
  7.7 5.6 %constant_dynamic-slice_fusion.13 = (bf16[1024,256]{1,0:T(8,128)(2,1)S(1)}, bf16[1024,256]{1,0:T(8,128)(2,1)}, bf16[1024,256]{1,0:T(8,128)(2,1)S(1)}, bf16[1024,...) fusion(bf16[1024,4096]{1,0:T(8,128)(2,1)} %param.8, ...), kind=kLoop, calls=%fused_computation.85 | loop fusion | bytes 16777280 | tf_op jit(solution)/shard_map/dynamic_slice | solution.py:33
  13.3 0.2 collective-permute-start.11
  13.5 19.8 %collective-permute-done.11 = bf16[1024,256]{1,0:T(8,128)(2,1)S(1)} collective-permute-done((bf16[1024,256]{1,0:T(8,128)(2,1)S(1)}, bf16[1024,256]{1,0:T(8,128)(2,1)S(1)}, u32[]{:S(2)}, u32[]{:S(2)}) %collective-permute-start.11) | collective-permute-done | bytes 524320 | tf_op jit(solution)/shard_map/ppermute | solution.py:37
  33.3 1.1 pad_maximum_fusion.8
  34.3 0.0 all-gather.19.cloned.1.call-start
  34.4 0.4 collective-permute-start.8
  34.8 1.7 collective-permute-done.8
  36.6 2.1 pad_maximum_fusion.6
  38.7 0.0 all-gather.15.cloned.1.call-start
  38.7 0.4 collective-permute-start.5
  39.2 1.7 collective-permute-done.5
  40.9 1.1 pad_maximum_fusion.4
  42.0 0.0 all-gather.11.cloned.1.call-start
  42.1 0.4 collective-permute-start.2
  42.5 1.7 collective-permute-done.2
  44.2 1.1 pad_maximum_fusion.2
  45.3 0.0 all-gather.21.cloned.1.call-start
  45.4 0.4 collective-permute-start.10
  45.8 1.7 collective-permute-done.10
  47.6 1.1 pad_maximum_fusion.7
  48.7 0.4 collective-permute-start.7
  49.2 1.5 collective-permute-done.7
  50.7 1.0 pad_maximum_fusion.5
  51.8 0.0 all-gather.13.cloned.1.call-start
  51.8 0.4 collective-permute-start.4
  52.3 1.5 collective-permute-done.4
  53.8 1.1 pad_maximum_fusion.3
  54.9 0.2 all-gather.9.cloned.1.call-start
  55.1 0.4 collective-permute-start
  55.6 1.5 collective-permute-done
  57.1 1.0 pad_maximum_fusion.1
  58.1 12.1 %all-gather.23.cloned.1.call-done = bf16[2048,512]{1,0:T(8,128)(2,1)} async-done(((bf16[1024,512]{1,0:T(8,128)(2,1)}), bf16[2048,512]{1,0:T(8,128)(2,1)}) %all-gather.23.cloned.1.call-update) | async-done | bytes 2097168 | tf_op jit(solution)/shard_map/all_gather | solution.py:39
  70.2 8.6 %fusion.20 = f32[256,4096]{1,0:T(8,128)S(1)} fusion(bf16[2048,4096]{1,0:T(8,128)(2,1)} %collective-permute-done.1, bf16[2048,512]{1,0:T(8,128)(2,1)} %all-gather.23.cloned.1.call-done), kind=kOutput, calls=%fused_computation.36 | convolution fusion | flops 4294967296 | bytes 22020096 | tf_op jit(solution)/shard_map/dot_general | solution.py:15
  78.8 12.4 %fusion.11 = bf16[256,4096]{1,0:T(8,128)(2,1)} fusion(f32[256,4096]{1,0:T(8,128)S(1)} %fusion.20, bf16[2048,4096]{1,0:T(8,128)(2,1)} %param.7, bf16[2048,512]{1,0:T(8,128)(2,1)S(1)} %copy-done), kind=kOutput, calls=%fused_computation.23 | convolution fusion | flops 4297064448 | bytes 24117248 | tf_op jit(solution)/shard_map/dot_general | solution.py:15
  91.3 1.6 collective-permute-start.12
  92.8 12.7 %all-gather.19.cloned.1.call-done = bf16[2048,512]{1,0:T(8,128)(2,1)} async-done(((bf16[1024,512]{1,0:T(8,128)(2,1)}), bf16[2048,512]{1,0:T(8,128)(2,1)}) %all-gather.19.cloned.1.call-update) | async-done | bytes 2097168 | tf_op jit(solution)/shard_map/all_gather | solution.py:39
  105.5 8.6 %fusion.26 = f32[256,4096]{1,0:T(8,128)S(1)} fusion(bf16[2048,4096]{1,0:T(8,128)(2,1)} %collective-permute-done.1, bf16[2048,512]{1,0:T(8,128)(2,1)} %all-gather.19.cloned.1.call-done), kind=kOutput, calls=%fused_computation.42 | convolution fusion | flops 4294967296 | bytes 22020096 | tf_op jit(solution)/shard_map/dot_general | solution.py:15
  114.1 12.2 %fusion.10 = bf16[256,4096]{1,0:T(8,128)(2,1)} fusion(f32[256,4096]{1,0:T(8,128)S(1)} %fusion.26, bf16[2048,4096]{1,0:T(8,128)(2,1)} %param.7, bf16[2048,512]{1,0:T(8,128)(2,1)S(1)} %copy-done.1), kind=kOutput, calls=%fused_computation.22 | convolution fusion | flops 4297064448 | bytes 24117248 | tf_op jit(solution)/shard_map/dot_general | solution.py:15
  126.3 1.6 collective-permute-start.9
  127.9 12.3 %all-gather.15.cloned.1.call-done = bf16[2048,512]{1,0:T(8,128)(2,1)} async-done(((bf16[1024,512]{1,0:T(8,128)(2,1)}), bf16[2048,512]{1,0:T(8,128)(2,1)}) %all-gather.15.cloned.1.call-update) | async-done | bytes 2097168 | tf_op jit(solution)/shard_map/all_gather | solution.py:39
  140.2 8.6 %fusion.32 = f32[256,4096]{1,0:T(8,128)S(1)} fusion(bf16[2048,4096]{1,0:T(8,128)(2,1)} %collective-permute-done.1, bf16[2048,512]{1,0:T(8,128)(2,1)} %all-gather.15.cloned.1.call-done), kind=kOutput, calls=%fused_computation.48 | convolution fusion | flops 4294967296 | bytes 22020096 | tf_op jit(solution)/shard_map/dot_general | solution.py:15
  148.8 12.3 %fusion.9 = bf16[256,4096]{1,0:T(8,128)(2,1)} fusion(f32[256,4096]{1,0:T(8,128)S(1)} %fusion.32, bf16[2048,4096]{1,0:T(8,128)(2,1)} %param.7, bf16[2048,512]{1,0:T(8,128)(2,1)S(1)} %copy-done.2), kind=kOutput, calls=%fused_computation.21 | convolution fusion | flops 4297064448 | bytes 24117248 | tf_op jit(solution)/shard_map/dot_general | solution.py:15
  161.1 1.6 collective-permute-start.6
  162.7 12.1 %all-gather.11.cloned.1.call-done = bf16[2048,512]{1,0:T(8,128)(2,1)} async-done(((bf16[1024,512]{1,0:T(8,128)(2,1)}), bf16[2048,512]{1,0:T(8,128)(2,1)}) %all-gather.11.cloned.1.call-update) | async-done | bytes 2097168 | tf_op jit(solution)/shard_map/all_gather | solution.py:39
  174.8 8.6 %fusion.38 = f32[256,4096]{1,0:T(8,128)S(1)} fusion(bf16[2048,4096]{1,0:T(8,128)(2,1)} %collective-permute-done.1, bf16[2048,512]{1,0:T(8,128)(2,1)} %all-gather.11.cloned.1.call-done), kind=kOutput, calls=%fused_computation.54 | convolution fusion | flops 4294967296 | bytes 22020096 | tf_op jit(solution)/shard_map/dot_general | solution.py:15
  183.4 12.7 %fusion.8 = bf16[256,4096]{1,0:T(8,128)(2,1)} fusion(f32[256,4096]{1,0:T(8,128)S(1)} %fusion.38, bf16[2048,4096]{1,0:T(8,128)(2,1)} %param.7, bf16[2048,512]{1,0:T(8,128)(2,1)S(1)} %copy-done.3), kind=kOutput, calls=%fused_computation.20 | convolution fusion | flops 4297064448 | bytes 24117248 | tf_op jit(solution)/shard_map/dot_general | solution.py:15
  196.1 1.6 collective-permute-start.3
  197.7 12.2 %all-gather.21.cloned.1.call-done = bf16[2048,512]{1,0:T(8,128)(2,1)} async-done(((bf16[1024,512]{1,0:T(8,128)(2,1)}), bf16[2048,512]{1,0:T(8,128)(2,1)}) %all-gather.21.cloned.1.call-update) | async-done | bytes 2097168 | tf_op jit(solution)/shard_map/all_gather | solution.py:39
  209.9 12.7 %fusion.23 = f32[256,4096]{1,0:T(8,128)} fusion(bf16[2048,4096]{1,0:T(8,128)(2,1)} %collective-permute-done.1, bf16[2048,512]{1,0:T(8,128)(2,1)} %all-gather.21.cloned.1.call-done), kind=kOutput, calls=%fused_computation.39 | convolution fusion | flops 4294967296 | bytes 22020096 | tf_op jit(solution)/shard_map/dot_general | solution.py:15
  222.6 21.9 %all-gather.17.cloned.1.call-done = bf16[2048,512]{1,0:T(8,128)(2,1)} async-done(((bf16[1024,512]{1,0:T(8,128)(2,1)}), bf16[2048,512]{1,0:T(8,128)(2,1)}) %all-gather.17.cloned.1.call-update) | async-done | bytes 2097168 | tf_op jit(solution)/shard_map/all_gather | solution.py:39
  244.4 12.7 %fusion.29 = f32[256,4096]{1,0:T(8,128)} fusion(bf16[2048,4096]{1,0:T(8,128)(2,1)} %collective-permute-done.1, bf16[2048,512]{1,0:T(8,128)(2,1)} %all-gather.17.cloned.1.call-done), kind=kOutput, calls=%fused_computation.45 | convolution fusion | flops 4294967296 | bytes 22020096 | tf_op jit(solution)/shard_map/dot_general | solution.py:15
  257.1 22.0 %all-gather.13.cloned.1.call-done = bf16[2048,512]{1,0:T(8,128)(2,1)} async-done(((bf16[1024,512]{1,0:T(8,128)(2,1)}), bf16[2048,512]{1,0:T(8,128)(2,1)}) %all-gather.13.cloned.1.call-update) | async-done | bytes 2097168 | tf_op jit(solution)/shard_map/all_gather | solution.py:39
  279.1 12.9 %fusion.35 = f32[256,4096]{1,0:T(8,128)} fusion(bf16[2048,4096]{1,0:T(8,128)(2,1)} %collective-permute-done.1, bf16[2048,512]{1,0:T(8,128)(2,1)} %all-gather.13.cloned.1.call-done), kind=kOutput, calls=%fused_computation.51 | convolution fusion | flops 4294967296 | bytes 22020096 | tf_op jit(solution)/shard_map/dot_general | solution.py:15
  292.0 21.8 %all-gather.9.cloned.1.call-done = bf16[2048,512]{1,0:T(8,128)(2,1)} async-done(((bf16[1024,512]{1,0:T(8,128)(2,1)}), bf16[2048,512]{1,0:T(8,128)(2,1)}) %all-gather.9.cloned.1.call-update) | async-done | bytes 2097168 | tf_op jit(solution)/shard_map/all_gather | solution.py:39
  313.8 8.6 %fusion.41 = f32[256,4096]{1,0:T(8,128)S(1)} fusion(bf16[2048,4096]{1,0:T(8,128)(2,1)} %collective-permute-done.1, bf16[2048,512]{1,0:T(8,128)(2,1)} %all-gather.9.cloned.1.call-done), kind=kOutput, calls=%fused_computation.57 | convolution fusion | flops 4294967296 | bytes 22020096 | tf_op jit(solution)/shard_map/dot_general | solution.py:15
  322.5 15.4 %fusion.18 = (f32[4096]{0:T(1024)S(1)}, f32[256]{0:T(256)S(1)}, f32[256,4096]{1,0:T(8,128)}) fusion(bf16[256,4096]{1,0:T(8,128)(2,1)} %collective-permute-done.12, f32[256,4096]{1,0:T(8,128)} %fusion.23, bf16[2048,4096]{1,0:T(8,128)(2,1)} %param.7, bf16[2048,512]{1,0:T(8,128)(2,1)} %all-gather.21.cloned.1.call-done), kind=kOutput, calls=%fused_computation.34 | convolution fusion | flops 4303351808 | bytes 28328960 | tf_op jit(solution)/shard_map/dot_general | solution.py:15
  337.9 9.1 %fusion.16 = (f32[4096]{0:T(1024)S(1)}, f32[256]{0:T(256)S(1)}, f32[256,4096]{1,0:T(8,128)}) fusion(bf16[256,4096]{1,0:T(8,128)(2,1)} %collective-permute-done.9, f32[256,4096]{1,0:T(8,128)} %fusion.29, bf16[2048,4096]{1,0:T(8,128)(2,1)S(1)} %bitcast.17, bf16[2048,512]{1,0:T(8,128)(2,1)} %all-gather.17.cloned.1.call-done), kind=kOutput, calls=%fused_computation.32 | convolution fusion | flops 4303351808 | bytes 28328960 | tf_op jit(solution)/shard_map/dot_general | solution.py:15
  347.0 9.0 %fusion.14 = (f32[4096]{0:T(1024)S(1)}, f32[256]{0:T(256)S(1)}, f32[256,4096]{1,0:T(8,128)}) fusion(bf16[256,4096]{1,0:T(8,128)(2,1)} %collective-permute-done.6, f32[256,4096]{1,0:T(8,128)} %fusion.35, bf16[2048,4096]{1,0:T(8,128)(2,1)S(1)} %bitcast.17, bf16[2048,512]{1,0:T(8,128)(2,1)} %all-gather.13.cloned.1.call-done), kind=kOutput, calls=%fused_computation.30 | convolution fusion | flops 4303351808 | bytes 28328960 | tf_op jit(solution)/shard_map/dot_general | solution.py:15
  356.0 8.6 %fusion.12 = (f32[4096]{0:T(1024)S(1)}, f32[256]{0:T(256)S(1)}, f32[256,4096]{1,0:T(8,128)}) fusion(bf16[256,4096]{1,0:T(8,128)(2,1)} %collective-permute-done.3, f32[256,4096]{1,0:T(8,128)S(1)} %fusion.41, bf16[2048,4096]{1,0:T(8,128)(2,1)S(1)} %bitcast.17, bf16[2048,512]{1,0:T(8,128)(2,1)} %all-gather.9.cloned.1.call-done), kind=kOutput, calls=%fused_computation.28 | convolution fusion | flops 4303351808 | bytes 28328960 | tf_op jit(solution)/shard_map/dot_general | solution.py:15
  364.7 4.9 %psum.21 = f32[1024]{0:T(1024)S(1)} all-reduce(f32[1024]{0:T(1024)S(1)} %pad_maximum_fusion.9), channel_id=1, replica_groups=mesh['dp'=4,'row'=2,'col'=4] {'row'}, use_global_device_ids=true, to_apply=%region_4.5 | all-reduce | flops 1024 | bytes 8192 | tf_op jit(solution)/shard_map/psum | solution.py:60
  369.6 0.6 fusion.44
  370.2 60.4 %all-reduce = (f32[]{:T(128)}, f32[4096]{0:T(1024)S(1)}) all-reduce(f32[]{:T(128)} %get-tuple-element.17, f32[4096]{0:T(1024)S(1)} %add_add_fusion), channel_id=1, replica_groups=mesh['dp'=4,'row'=2,'col'=4] {'dp','col'}, use_global_device_ids=true, to_apply=%region_11.12 | all-reduce | flops 4097 | bytes 32776 | tf_op jit(solution)/shard_map/psum | solution.py:63
  431.3 32.6 %multiply_subtract_fusion.1 = (f32[1024,4096]{1,0:T(8,128)}, bf16[1024,4096]{1,0:T(8,128)(2,1)}, f32[1024,4096]{1,0:T(8,128)}) fusion(f32[1024,4096]{1,0:T(8,128)} %param.9, f32[]{:T(128)S(6)} %div.36, f32[4096]{0:T(1024)S(1)} %multiply_add_fusion.4, f32[1024]{0:T(1024)S(1)} %get-tuple-element.18, f32[256,4096]{1,0:T(8,128)} %get-tuple-element.36, ...), kind=kLoop, calls=%fused_computation.2 | loop fusion | flops 71303168 | bytes 100683776 | tf_op jit(solution)/shard_map/sub | solution.py:69
  (49 shorter events, 0.3 us)
Async XLA Ops:
  7.2 63.1 %all-gather.23.cloned.1.call-start = ((), (), s32[]{:S(2)}) async-start(), calls=%async_computation.7 | async-start | bytes 3145728 | tf_op jit(solution)/shard_map/all_gather | solution.py:39
  7.2 63.0 %collective-permute-start.1 = (bf16[2048,4096]{1,0:T(8,128)(2,1)}, bf16[2048,4096]{1,0:T(8,128)(2,1)}, u32[]{:S(2)}, u32[]{:S(2)}) collective-permute-start(bf16[2048,4096]{1,0:T(8,128)(2,1)} %param.7), channel_id=1, source_target_pairs={{0,8},{8,0},{16,24},{24,16},{1,9},{9,1},{17,25},{25,17},{2,10},{10... | collective-permute-start | bytes 50331656 | tf_op jit(solution)/shard_map/ppermute | solution.py:30
  13.3 20.0 %collective-permute-start.11 = (bf16[1024,256]{1,0:T(8,128)(2,1)S(1)}, bf16[1024,256]{1,0:T(8,128)(2,1)S(1)}, u32[]{:S(2)}, u32[]{:S(2)}) collective-permute-start(bf16[1024,256]{1,0:T(8,128)(2,1)S(1)} %get-tuple-element.34), channel_id=1, source_target_pairs={{0,8},{8,0},{16,24},{24,16},{1,9},{9,1},{17,25},{25,17},{2,10},{10... | collective-permute-start | bytes 1572872 | tf_op jit(solution)/shard_map/ppermute | solution.py:37
  34.3 71.2 %all-gather.19.cloned.1.call-start = ((), (), s32[]{:S(2)}) async-start(), calls=%async_computation.5 | async-start | bytes 3145728 | tf_op jit(solution)/shard_map/all_gather | solution.py:39
  34.4 2.2 collective-permute-start.8
  38.7 101.5 %all-gather.15.cloned.1.call-start = ((), (), s32[]{:S(2)}) async-start(), calls=%async_computation.3 | async-start | bytes 3145728 | tf_op jit(solution)/shard_map/all_gather | solution.py:39
  38.7 2.2 collective-permute-start.5
  42.0 6.7 %copy-start.6 = (bf16[1024,256]{1,0:T(8,128)(2,1)S(1)}, bf16[1024,256]{1,0:T(8,128)(2,1)}, u32[]{:S(2)}) copy-start(bf16[1024,256]{1,0:T(8,128)(2,1)} %get-tuple-element.25) | copy-start | bytes 1572868
  42.0 132.8 %all-gather.11.cloned.1.call-start = ((), (), s32[]{:S(2)}) async-start(), calls=%async_computation.1 | async-start | bytes 3145728 | tf_op jit(solution)/shard_map/all_gather | solution.py:39
  42.1 2.2 collective-permute-start.2
  45.3 6.5 %copy-start.5 = (bf16[1024,256]{1,0:T(8,128)(2,1)S(1)}, bf16[1024,256]{1,0:T(8,128)(2,1)}, u32[]{:S(2)}) copy-start(bf16[1024,256]{1,0:T(8,128)(2,1)} %get-tuple-element.29) | copy-start | bytes 1572868
  45.3 164.5 %all-gather.21.cloned.1.call-start = ((), (), s32[]{:S(2)}) async-start(), calls=%async_computation.6 | async-start | bytes 3145728 | tf_op jit(solution)/shard_map/all_gather | solution.py:39
  45.4 2.2 collective-permute-start.10
  48.6 6.5 %copy-start.4 = (bf16[1024,256]{1,0:T(8,128)(2,1)S(1)}, bf16[1024,256]{1,0:T(8,128)(2,1)}, u32[]{:S(2)}) copy-start(bf16[1024,256]{1,0:T(8,128)(2,1)} %get-tuple-element.32) | copy-start | bytes 1572868
  48.7 195.8 %all-gather.17.cloned.1.call-start = ((), (), s32[]{:S(2)}) async-start(), calls=%async_computation.4 | async-start | bytes 3145728 | tf_op jit(solution)/shard_map/all_gather | solution.py:39
  48.7 2.0 collective-permute-start.7
  51.8 227.4 %all-gather.13.cloned.1.call-start = ((), (), s32[]{:S(2)}) async-start(), calls=%async_computation.2 | async-start | bytes 3145728 | tf_op jit(solution)/shard_map/all_gather | solution.py:39
  51.8 2.0 collective-permute-start.4
  54.9 258.9 %all-gather.9.cloned.1.call-start = ((), (), s32[]{:S(2)}) async-start(), calls=%async_computation | async-start | bytes 3145728 | tf_op jit(solution)/shard_map/all_gather | solution.py:39
  55.1 2.0 collective-permute-start
  70.2 8.6 %copy-start = (bf16[2048,512]{1,0:T(8,128)(2,1)S(1)}, bf16[2048,512]{1,0:T(8,128)(2,1)}, u32[]{:S(2)}) copy-start(bf16[2048,512]{1,0:T(8,128)(2,1)} %all-gather.23.cloned.1.call-done) | copy-start | bytes 6291460
  91.3 231.2 %collective-permute-start.12 = (bf16[256,4096]{1,0:T(8,128)(2,1)}, bf16[256,4096]{1,0:T(8,128)(2,1)}, u32[]{:S(2)}, u32[]{:S(2)}) collective-permute-start(bf16[256,4096]{1,0:T(8,128)(2,1)} %fusion.11), channel_id=1, source_target_pairs={{0,16},{8,24},{16,0},{24,8},{1,17},{9,25},{17,1},{25,9},{2,18},{10... | collective-permute-start | bytes 6291464 | tf_op jit(solution)/shard_map/ppermute | solution.py:49
  105.5 8.6 %copy-start.1 = (bf16[2048,512]{1,0:T(8,128)(2,1)S(1)}, bf16[2048,512]{1,0:T(8,128)(2,1)}, u32[]{:S(2)}) copy-start(bf16[2048,512]{1,0:T(8,128)(2,1)} %all-gather.19.cloned.1.call-done) | copy-start | bytes 6291460
  126.3 211.6 %collective-permute-start.9 = (bf16[256,4096]{1,0:T(8,128)(2,1)}, bf16[256,4096]{1,0:T(8,128)(2,1)}, u32[]{:S(2)}, u32[]{:S(2)}) collective-permute-start(bf16[256,4096]{1,0:T(8,128)(2,1)} %fusion.10), channel_id=1, source_target_pairs={{0,16},{8,24},{16,0},{24,8},{1,17},{9,25},{17,1},{25,9},{2,18},{10... | collective-permute-start | bytes 6291464 | tf_op jit(solution)/shard_map/ppermute | solution.py:49
  140.2 8.6 %copy-start.2 = (bf16[2048,512]{1,0:T(8,128)(2,1)S(1)}, bf16[2048,512]{1,0:T(8,128)(2,1)}, u32[]{:S(2)}) copy-start(bf16[2048,512]{1,0:T(8,128)(2,1)} %all-gather.15.cloned.1.call-done) | copy-start | bytes 6291460
  161.1 185.9 %collective-permute-start.6 = (bf16[256,4096]{1,0:T(8,128)(2,1)}, bf16[256,4096]{1,0:T(8,128)(2,1)}, u32[]{:S(2)}, u32[]{:S(2)}) collective-permute-start(bf16[256,4096]{1,0:T(8,128)(2,1)} %fusion.9), channel_id=1, source_target_pairs={{0,16},{8,24},{16,0},{24,8},{1,17},{9,25},{17,1},{25,9},{2,18},{10... | collective-permute-start | bytes 6291464 | tf_op jit(solution)/shard_map/ppermute | solution.py:49
  174.8 8.6 %copy-start.3 = (bf16[2048,512]{1,0:T(8,128)(2,1)S(1)}, bf16[2048,512]{1,0:T(8,128)(2,1)}, u32[]{:S(2)}) copy-start(bf16[2048,512]{1,0:T(8,128)(2,1)} %all-gather.11.cloned.1.call-done) | copy-start | bytes 6291460
  196.1 160.0 %collective-permute-start.3 = (bf16[256,4096]{1,0:T(8,128)(2,1)}, bf16[256,4096]{1,0:T(8,128)(2,1)}, u32[]{:S(2)}, u32[]{:S(2)}) collective-permute-start(bf16[256,4096]{1,0:T(8,128)(2,1)} %fusion.8), channel_id=1, source_target_pairs={{0,16},{8,24},{16,0},{24,8},{1,17},{9,25},{17,1},{25,9},{2,18},{10... | collective-permute-start | bytes 6291464 | tf_op jit(solution)/shard_map/ppermute | solution.py:49
  313.8 24.1 %slice-start = ((s8[16777216]{0:T(1024)(128)(4,1)}), s8[4194304]{0:T(1024)(128)(4,1)S(1)}, s32[]{:S(2)}) async-start(s8[16777216]{0:T(1024)(128)(4,1)} %bitcast.16), calls=%async_computation.8 | async-start | bytes 8388608
  313.8 24.1 %slice-start.1 = ((s8[16777216]{0:T(1024)(128)(4,1)}), s8[4194304]{0:T(1024)(128)(4,1)S(1)}, s32[]{:S(2)}) async-start(s8[16777216]{0:T(1024)(128)(4,1)} %bitcast.16), calls=%async_computation.9 | async-start | bytes 8388608
  322.4 15.5 %slice-start.2 = ((s8[16777216]{0:T(1024)(128)(4,1)}), s8[4194304]{0:T(1024)(128)(4,1)S(1)}, s32[]{:S(2)}) async-start(s8[16777216]{0:T(1024)(128)(4,1)} %bitcast.16), calls=%async_computation.10 | async-start | bytes 8388608
  322.4 15.5 %slice-start.3 = ((s8[16777216]{0:T(1024)(128)(4,1)}), s8[4194304]{0:T(1024)(128)(4,1)S(1)}, s32[]{:S(2)}) async-start(s8[16777216]{0:T(1024)(128)(4,1)} %bitcast.16), calls=%async_computation.11 | async-start | bytes 8388608
  356.0 13.6 %copy-start.10 = (f32[1024]{0:T(1024)S(1)}, f32[1024]{0:T(1024)}, u32[]{:S(2)}) copy-start(f32[1024]{0:T(1024)} %param.12) | copy-start | bytes 12292
  356.0 75.2 %copy-start.9 = (f32[4096]{0:T(1024)S(1)}, f32[4096]{0:T(1024)}, u32[]{:S(2)}) copy-start(f32[4096]{0:T(1024)} %param.13) | copy-start | bytes 49156
  370.2 93.6 %copy-start.8 = (f32[1024]{0:T(1024)}, f32[1024]{0:T(1024)S(1)}, u32[]{:S(2)}) copy-start(f32[1024]{0:T(1024)S(1)} %get-tuple-element.18) | copy-start | bytes 12292
  431.3 32.6 %copy-start.7 = (f32[4096]{0:T(1024)}, f32[4096]{0:T(1024)S(1)}, u32[]{:S(2)}) copy-start(f32[4096]{0:T(1024)S(1)} %multiply_add_fusion.4) | copy-start | bytes 49156
Sparse Core Ops, SparseCore 0:
  34.5 35.7 all-gather.22
  72.3 33.1 all-gather.18
  107.1 33.1 all-gather.14
  141.6 33.1 all-gather.10
  176.7 33.1 all-gather.20
  211.3 33.1 all-gather.16
  246.0 33.1 all-gather.12
  280.7 33.1 all-gather.8
